TPU v7x, 32 devices: a whole 2x2x4 slice. The times are simulated.
32 devices in a mesh: blk: 16 (over z, y, core), pair: 2 (over x).
Axes of the slice: x: 2, y: 2, z: 4, core: 2. Of those that a mesh axis runs over, the one named last changes fastest.
Arguments:
- particles: float32 [32768, 512], P(('blk', 'pair'))
- log_prior: float32 [32768], P(('blk', 'pair'))
- transition: bfloat16 [512, 512], replicated, may hold values from -0.25 to 0.25
- drive_vector: float32 [512], replicated, may hold values from -3 to 3
- current: float32 [4], replicated, may hold values from -4 to 4
- decay_rate: float32 [512], replicated, may hold values from 0.3 to 0.98
- obs_matrix: bfloat16 [512, 128], replicated, may hold values from -0.25 to 0.25
- obs_weight: float32 [128], replicated, may hold values from 0.05 to 0.5
- observed: float32 [4, 128], replicated
- ancestors: int32 [32768], P(('blk', 'pair')), may hold values from 0 to 1023
- cycle_pick: int32 [8192], P(('blk', 'pair')), may hold values from 0 to 1023, as said below
- pair_pick: int32 [1024], P(('blk', 'pair')), may hold values from 0 to 1023, as said below
Outputs:
- migrated: float32 [32768, 512], P(('blk', 'pair'))
- group_logw: float32 [32768], P(('blk', 'pair'))
- mean_state: float32 [512], replicated
Inputs may be any that keep to these rules, and one draw needn't show every extreme that they name: On each device, cycle_pick's 256 entries and pair_pick's 32 entries are distinct local positions, none shared between the two. `pair_pick`: distinct local positions, none in the same device's cycle_pick.
All inputs are finite; a program needn't handle non-finite values.
Results may differ from a plain program's by a relative error of at most 0.013.
Values sent between devices are 32-bit elements; how exact they have to be, the bound alone decides.
A program may use at most 64 MiB of HBM per device.

v0:
```python
import jax
import jax.numpy as jnp
from jax import lax
from jax.sharding import PartitionSpec as P

STEPS = 4


def shifted(block, axis, distance):
    devices = range(lax.axis_size(axis))
    route = [((i - distance) % len(devices), i) for i in devices]
    return lax.ppermute(block, axis, route)


def per_device(
    particles,
    log_prior,
    transition,
    drive_vector,
    current,
    decay_rate,
    obs_matrix,
    obs_weight,
    observed,
    ancestors,
    cycle_pick,
    pair_pick,
):
    state = particles
    logw = log_prior
    rounded = state.astype(jnp.bfloat16)
    for step_index in range(STEPS):
        drift = (
            jnp.dot(rounded, transition, preferred_element_type=jnp.float32)
            + current[step_index] * drive_vector
        )
        state = decay_rate * state + jnp.tanh(drift)
        rounded = state.astype(jnp.bfloat16)
        predicted = jnp.dot(rounded, obs_matrix, preferred_element_type=jnp.float32)
        misfit = predicted - observed[step_index]
        logw = logw - 0.5 * jnp.sum(obs_weight * misfit * misfit, axis=1)
    groups = lax.axis_size("blk") * lax.axis_size("pair")
    rows_here = state.shape[0]
    resampled = state[ancestors]
    cycle_sent = resampled[cycle_pick]
    pair_sent = resampled[pair_pick]
    peak = lax.pmax(jnp.max(logw), ("blk", "pair"))
    expw = jnp.exp(logw - peak)
    local_sum = jnp.sum(expw)
    weighted = jnp.dot(expw, state, precision=lax.Precision.HIGHEST)
    total, summed = lax.psum((local_sum, weighted), ("blk", "pair"))
    mean_state = summed / total
    dev_logw = jnp.log(jnp.maximum(groups * local_sum / total, 0.1))
    weight_cell = jnp.reshape(dev_logw, (1,))
    cycle_in, cycle_w = shifted((cycle_sent, weight_cell), "blk", 1)
    half_pair = lax.axis_size("pair") // 2
    pair_in, pair_w = shifted((pair_sent, weight_cell), "pair", half_pair)
    migrated = resampled.at[cycle_pick].set(cycle_in).at[pair_pick].set(pair_in)
    base_w = jnp.full((rows_here,), dev_logw, jnp.float32)
    group_logw = base_w.at[cycle_pick].set(cycle_w[0]).at[pair_pick].set(pair_w[0])
    return (migrated, group_logw, mean_state)


def solution(mesh):
    placed = (
        P(("blk", "pair"), None),
        P(("blk", "pair")),
        P(),
        P(),
        P(),
        P(),
        P(),
        P(),
        P(),
        P(("blk", "pair")),
        P(("blk", "pair")),
        P(("blk", "pair")),
    )
    return jax.shard_map(
        per_device,
        mesh=mesh,
        in_specs=placed,
        out_specs=(P(("blk", "pair"), None), P(("blk", "pair")), P()),
        check_vma=False,
    )
```

profile of v0, /device:TPU:0, one launch (start us, length us, event | category | flops | bytes accessed | tf_op | source)
XLA Modules:
  0.0 132.4 jit_solution(12886302946917916723)
XLA Ops:
  0.6 1.5 %fusion.21 = (f32[1]{0:T(128)}, f32[1]{0:T(128)}, f32[1]{0:T(128)}, f32[1]{0:T(128)}) fusion(f32[4]{0:T(128)} %param.16), kind=kLoop, calls=%fused_computation.52 | loop fusion | bytes 32 | tf_op jit(solution)/shard_map/slice | solution.py:35
  2.1 0.8 slice_bitcast_fusion.3
  3.0 3.3 %broadcast_multiply_fusion = (f32[512]{0:T(512)S(1)}, f32[512]{0:T(512)S(1)}, f32[512]{0:T(512)S(1)}, f32[512]{0:T(512)S(1)}) fusion(f32[512]{0:T(512)} %param.15, f32[]{:T(128)} %bitcast.3, f32[]{:T(128)} %bitcast.1, f32[]{:T(128)} %bitcast, f32[]{:T(128)} %bitcast.2), kind=kLoop, calls=%fused_computation.42 | loop fusion | flops 2048 | bytes 10256 | tf_op jit(solution)/shard_map/mul | solution.py:35
  6.3 3.0 %tanh_add_fusion.3 = f32[1024,512]{1,0:T(8,128)S(1)} fusion(f32[1024,512]{1,0:T(8,128)} %param.12, bf16[512,512]{1,0:T(8,128)(2,1)S(1)} %copy-done, f32[512]{0:T(512)S(1)} %get-tuple-element.15, f32[512]{0:T(512)} %param.17), kind=kOutput, calls=%fused_computation.10 | convolution fusion | flops 538968064 | bytes 4722688 | tf_op jit(solution)/shard_map/dot_general | solution.py:34
  9.3 0.7 tanh_add_fusion.2
  11.2 0.7 tanh_add_fusion.1
  12.4 0.7 tanh_add_fusion
  14.5 42.1 %pmax.7 = f32[]{:T(128)} all-reduce(f32[]{:T(128)} %get-tuple-element.7), channel_id=1, replica_groups=mesh['blk'=16,'pair'=2] {'blk','pair'}, use_global_device_ids=true, to_apply=%region_7.0 | all-reduce | flops 1 | bytes 8 | tf_op jit(solution)/shard_map/pmax | solution.py:47
  56.6 1.3 fusion.19
  57.8 1.1 fusion.22
  59.6 40.6 %all-reduce = (f32[]{:T(128)}, f32[512]{0:T(512)S(1)}) all-reduce(f32[]{:T(128)} %get-tuple-element.5, f32[512]{0:T(512)S(1)} %bitcast.32), channel_id=1, replica_groups=mesh['blk'=16,'pair'=2] {'blk','pair'}, use_global_device_ids=true, to_apply=%region_9.0 | all-reduce | flops 513 | bytes 4104 | tf_op jit(solution)/shard_map/psum | solution.py:51
  100.9 3.6 %collective-permute-start.3 = (f32[1]{0:T(128)}, f32[1]{0:T(128)}, u32[]{:S(2)}, u32[]{:S(2)}) collective-permute-start(f32[1]{0:T(128)} %bitcast.8), channel_id=1, source_target_pairs={{1,0},{0,1},{3,2},{2,3},{5,4},{4,5},{7,6},{6,7},{9,8},{8,9},{11,10... | collective-permute-start | bytes 20 | tf_op jit(solution)/shard_map/ppermute | solution.py:12
  104.6 1.0 collective-permute-start.2
  105.6 4.9 %gather_fusion = f32[1024,512]{1,0:T(8,128)} fusion(f32[1024,512]{1,0:T(8,128)S(1)} %tanh_add_fusion, s32[1024]{0:T(1024)S(1)} %fusion.16), kind=kCustom, calls=%fused_computation | custom fusion | bytes 4198400 | tf_op jit(solution)/shard_map/gather | solution.py:44
  110.4 2.8 %gather_fusion.1 = f32[256,512]{1,0:T(8,128)S(1)} fusion(f32[1024,512]{1,0:T(8,128)} %gather_fusion, s32[1024]{0:T(1024)S(1)} %pad_clamp_fusion.1), kind=kCustom, calls=%fused_computation.1 | custom fusion | bytes 1049600 | tf_op jit(solution)/shard_map/gather | solution.py:45
  113.2 1.6 %collective-permute-start = (f32[256,512]{1,0:T(8,128)S(1)}, f32[256,512]{1,0:T(8,128)S(1)}, u32[]{:S(2)}, u32[]{:S(2)}) collective-permute-start(f32[256,512]{1,0:T(8,128)S(1)} %gather_fusion.1), channel_id=1, source_target_pairs={{30,0},{0,2},{2,4},{4,6},{6,8},{8,10},{10,12},{12,14},{14,16},{16,... | collective-permute-start | bytes 1572872 | tf_op jit(solution)/shard_map/ppermute | solution.py:12
  114.9 2.2 %gather_fusion.2 = f32[32,512]{1,0:T(8,128)S(1)} fusion(f32[1024,512]{1,0:T(8,128)} %gather_fusion, s32[1024]{0:T(1024)S(1)} %pad_clamp_fusion), kind=kCustom, calls=%fused_computation.2 | custom fusion | bytes 131200 | tf_op jit(solution)/shard_map/gather | solution.py:46
  117.7 1.2 broadcast_divide_fusion
  118.9 0.6 broadcast.26
  119.6 1.4 %scatter_custom_fusion.2 = f32[1024]{0:T(1024)S(1)} fusion(s32[256]{0:T(256)S(1)} %compare_select_fusion.1, f32[256]{0:T(256)S(1)} %broadcast.26, f32[]{:T(128)} %log.3), kind=kCustom, calls=%fused_computation.39 | custom fusion | bytes 4100 | tf_op jit(solution)/shard_map/scatter | solution.py:60
  121.6 0.7 scatter_fusion.2
  122.3 2.3 %collective-permute-done = f32[256,512]{1,0:T(8,128)S(1)} collective-permute-done((f32[256,512]{1,0:T(8,128)S(1)}, f32[256,512]{1,0:T(8,128)S(1)}, u32[]{:S(2)}, u32[]{:S(2)}) %collective-permute-start) | collective-permute-done | bytes 524320 | tf_op jit(solution)/shard_map/ppermute | solution.py:12
  124.6 4.3 %scatter_fusion = f32[1024,512]{1,0:T(8,128)} fusion(f32[1024,512]{1,0:T(8,128)} %gather_fusion, s32[256]{0:T(256)S(1)} %compare_select_fusion.1, f32[256,512]{1,0:T(8,128)S(1)} %collective-permute-done), kind=kCustom, calls=%fused_computation.3 | custom fusion | bytes 1573888 | tf_op jit(solution)/shard_map/scatter | solution.py:58
  128.9 3.6 %scatter_fusion.1 = f32[1024,512]{1,0:T(8,128)} fusion(f32[1024,512]{1,0:T(8,128)} %scatter_fusion, s32[32]{0:T(128)S(1)} %compare_select_fusion.2, f32[32,512]{1,0:T(8,128)S(1)} %collective-permute-done.1), kind=kCustom, calls=%fused_computation.4 | custom fusion | bytes 196736 | tf_op jit(solution)/shard_map/scatter | solution.py:58
  (33 shorter events, 4.1 us)
Async XLA Ops:
  0.6 5.6 %copy-start = (bf16[512,512]{1,0:T(8,128)(2,1)S(1)}, bf16[512,512]{1,0:T(8,128)(2,1)}, u32[]{:S(2)}) copy-start(bf16[512,512]{1,0:T(8,128)(2,1)} %param.14) | copy-start | bytes 1572868
  6.3 3.0 %copy-start.7 = (f32[512]{0:T(512)S(1)}, f32[512]{0:T(512)}, u32[]{:S(2)}) copy-start(f32[512]{0:T(512)} %param.17) | copy-start | bytes 6148
  9.3 0.9 copy-start.2
  9.3 0.9 copy-start.3
  13.2 0.7 copy-start.4
  13.2 92.3 %copy-start.6 = (s32[256]{0:T(256)S(1)}, s32[256]{0:T(256)}, u32[]{:S(2)}) copy-start(s32[256]{0:T(256)} %param.22) | copy-start | bytes 3076
  13.2 92.3 %copy-start.5 = (s32[1024]{0:T(1024)S(1)}, s32[1024]{0:T(1024)}, u32[]{:S(2)}) copy-start(s32[1024]{0:T(1024)} %param.21) | copy-start | bytes 12292
  100.9 20.1 %collective-permute-start.3 = (f32[1]{0:T(128)}, f32[1]{0:T(128)}, u32[]{:S(2)}, u32[]{:S(2)}) collective-permute-start(f32[1]{0:T(128)} %bitcast.8), channel_id=1, source_target_pairs={{1,0},{0,1},{3,2},{2,3},{5,4},{4,5},{7,6},{6,7},{9,8},{8,9},{11,10... | collective-permute-start | bytes 20 | tf_op jit(solution)/shard_map/ppermute | solution.py:12
  104.6 14.4 %collective-permute-start.2 = (f32[1]{0:T(128)}, f32[1]{0:T(128)}, u32[]{:S(2)}, u32[]{:S(2)}) collective-permute-start(f32[1]{0:T(128)} %bitcast.8), channel_id=1, source_target_pairs={{30,0},{0,2},{2,4},{4,6},{6,8},{8,10},{10,12},{12,14},{14,16},{16,... | collective-permute-start | bytes 20 | tf_op jit(solution)/shard_map/ppermute | solution.py:12
  110.4 4.4 %copy-start.8 = (s32[32]{0:T(128)S(1)}, s32[32]{0:T(128)}, u32[]{:S(2)}) copy-start(s32[32]{0:T(128)} %param.23) | copy-start | bytes 388
  113.2 11.4 %collective-permute-start = (f32[256,512]{1,0:T(8,128)S(1)}, f32[256,512]{1,0:T(8,128)S(1)}, u32[]{:S(2)}, u32[]{:S(2)}) collective-permute-start(f32[256,512]{1,0:T(8,128)S(1)} %gather_fusion.1), channel_id=1, source_target_pairs={{30,0},{0,2},{2,4},{4,6},{6,8},{8,10},{10,12},{12,14},{14,16},{16,... | collective-permute-start | bytes 1572872 | tf_op jit(solution)/shard_map/ppermute | solution.py:12
  117.1 11.8 %collective-permute-start.1 = (f32[32,512]{1,0:T(8,128)S(1)}, f32[32,512]{1,0:T(8,128)S(1)}, u32[]{:S(2)}, u32[]{:S(2)}) collective-permute-start(f32[32,512]{1,0:T(8,128)S(1)} %gather_fusion.2), channel_id=1, source_target_pairs={{1,0},{0,1},{3,2},{2,3},{5,4},{4,5},{7,6},{6,7},{9,8},{8,9},{11,10... | collective-permute-start | bytes 196616 | tf_op jit(solution)/shard_map/ppermute | solution.py:12
  122.2 6.6 %copy-start.1 = (f32[1024]{0:T(1024)}, f32[1024]{0:T(1024)S(1)}, u32[]{:S(2)}) copy-start(f32[1024]{0:T(1024)S(1)} %scatter_fusion.2) | copy-start | bytes 12292
where the time goes:
time: 133 us; the launch traced here: 132 us
  blocking collectives  82.7 us (62%)
  local copies, waits for them, and re-layouts  23.7 us (18%)
  matrix products  8.26 us (6%)
  starting transfers between devices  6.8 us (5%)
  other arithmetic  6.42 us (5%)
  waiting for transfers between devices  2.34 us (2%)
  between operations  2.23 us (2%)
    pmax x1, blocking collectives, per_device(): peak = lax.pmax(jnp.max(logw), ('blk', 'pair'))  42.1 us
    psum x1, blocking collectives, per_device(): total, summed = lax.psum((local_sum, weighted), ('blk', 'pair'))  40.6 us
    scatter x2, local copies, waits for them, and re-layouts, per_device(): migrated = resampled.at[cycle_pick].set(cycle_in).at[pair_pick].set(pair_in)  7.84 us
    ppermute x4, starting transfers between devices, shifted(): return lax.ppermute(block, axis, route)  6.8 us
    dot_general x4, matrix products, per_device(): jnp.dot(rounded, transition, preferred_element_type=jnp.float32)  5.18 us
    gather x1, local copies, waits for them, and re-layouts, per_device(): resampled = state[ancestors]  4.87 us
    mul x1, other arithmetic, per_device(): current[step_index] * drive_vector  3.31 us
    gather x1, local copies, waits for them, and re-layouts, per_device(): cycle_sent = resampled[cycle_pick]  2.81 us
  transfers between devices with their start and end apart: 4, of which 1 were waited for; matrix products, arithmetic and copies ran while one was open for 14% of the time, Pallas kernels for 0%

commit v1 on v0

v1 whole, which is shorter than its diff:
```python
import functools

import jax
import jax.numpy as jnp
from jax import lax
from jax.experimental import pallas as pl
from jax.experimental.pallas import tpu as pltpu
from jax.sharding import PartitionSpec as P

MESH = pl.DeviceIdType.MESH
F32 = jnp.float32
BF16 = jnp.bfloat16
LANES = 128
CHUNK = 256


def column(row_block):
    rows = jnp.broadcast_to(row_block, (8, row_block.shape[1]))
    return rows.T[:, 0:1]


def kernel(
    nb,
    npair,
    part_hbm,
    prior_ref,
    trans_hbm,
    drive_ref,
    cur_ref,
    decay_ref,
    obsm_hbm,
    weight_ref,
    obs_ref,
    anc_ref,
    cyc_ref,
    pair_ref,
    out_ref,
    glw_ref,
    mean_ref,
    state,
    hi,
    lo,
    trans,
    obsm,
    acc,
    pick,
    pick_in,
    rout,
    rin,
    rhi,
    rlo,
    stats,
    load_sem,
    send_sem,
    recv_sem,
    stat_send,
    stat_recv,
):
    n = nb * npair
    b = lax.axis_index("blk")
    p = lax.axis_index("pair")
    me = b * npair + p
    rows, width = state.shape
    blocks = rows // LANES
    steps = obs_ref.shape[0]
    n_cyc = cyc_ref.shape[0] * LANES
    n_pair = pair_ref.shape[1]
    n_in = n_cyc + n_pair
    n_pad = rin.shape[0]

    loads = []
    for c in range(rows // CHUNK):
        part = pl.ds(c * CHUNK, CHUNK)
        loads.append(
            pltpu.make_async_copy(part_hbm.at[part], state.at[part], load_sem.at[c])
        )
    load_t = pltpu.make_async_copy(trans_hbm, trans, load_sem.at[len(loads)])
    load_o = pltpu.make_async_copy(obsm_hbm, obsm, load_sem.at[len(loads) + 1])
    for copy in loads:
        copy.start()
    load_t.start()
    load_o.start()

    barrier = pltpu.get_barrier_semaphore()

    def greet(k, carry):
        other = lax.rem(me + k, n)
        pl.semaphore_signal(
            barrier,
            inc=1,
            device_id=(other // npair, lax.rem(other, npair)),
            device_id_type=MESH,
        )
        return carry

    lax.fori_loop(1, n, greet, 0)

    anc = anc_ref[...].astype(F32)
    picks = [column(cyc_ref[q : q + 1, :].astype(F32)) for q in range(n_cyc // LANES)]
    picks.append(column(pair_ref[...].astype(F32)))
    pick_col = jnp.concatenate(picks, axis=0)
    lane = lax.broadcasted_iota(jnp.int32, (1, LANES), 1).astype(F32)
    place = lax.broadcasted_iota(jnp.int32, (n_in, 1), 0).astype(F32) + float(rows)
    parent = jnp.zeros((n_in, LANES), F32)
    source = []
    for r in range(blocks):
        hit = pick_col == lane + float(r * LANES)
        parent = parent + jnp.where(hit, anc[r : r + 1, :], 0.0)
        moved = jnp.sum(jnp.where(hit, place, 0.0), axis=0, keepdims=True)
        source.append(jnp.where(moved > 0.0, moved, anc[r : r + 1, :]))
    parent = jnp.sum(parent, axis=1, keepdims=True)
    source = jnp.concatenate(source, axis=0)
    wide = lax.broadcasted_iota(jnp.int32, (1, rows), 1).astype(F32)
    take = jnp.where(parent == wide, 1.0, 0.0).astype(BF16)

    sent = jnp.zeros((n_in, width), F32)
    for c, copy in enumerate(loads):
        copy.wait()
        part = slice(c * CHUNK, (c + 1) * CHUNK)
        hi[part, :] = state[part, :].astype(BF16)
        sent = sent + jnp.dot(take[:, part], hi[part, :], preferred_element_type=F32)
    rout[...] = sent

    pl.semaphore_wait(barrier, n - 1)
    right = lax.rem(b + 1, nb)
    across = lax.rem(p + npair // 2, npair)
    half = n_cyc // 2
    spans = [(0, half, (right, p)), (half, half, (right, p)), (n_cyc, n_pair, (b, across))]
    moves = []
    for q, (start, size, target) in enumerate(spans):
        part = pl.ds(start, size)
        move = pltpu.make_async_remote_copy(
            src_ref=rout.at[part],
            dst_ref=rin.at[part],
            send_sem=send_sem.at[q],
            recv_sem=recv_sem.at[q],
            device_id=target,
            device_id_type=MESH,
        )
        move.start()
        moves.append(move)

    load_t.wait()
    load_o.wait()
    decay = decay_ref[...]

    def advance(t, st, h, l, part):
        drift = jnp.dot(h[part, :], trans[...], preferred_element_type=F32)
        drift = drift + cur_ref[t] * drive_ref[...]
        new = decay * st[part, :] + jnp.tanh(drift)
        rounded = new.astype(BF16)
        st[part, :] = new
        h[part, :] = rounded
        if t == steps - 1:
            l[part, :] = (new - rounded.astype(F32)).astype(BF16)
        return rounded

    for t in range(steps):
        for c in range(rows // CHUNK):
            part = slice(c * CHUNK, (c + 1) * CHUNK)
            rounded = advance(t, state, hi, lo, part)
            predicted = jnp.dot(rounded, obsm[...], preferred_element_type=F32)
            misfit = predicted - obs_ref[t : t + 1, :]
            cost = weight_ref[...] * misfit * misfit
            if t:
                cost = cost + acc[part, :]
            acc[part, :] = cost

    prior_t = prior_ref[...].T
    logw = []
    for r in range(blocks):
        part = slice(r * LANES, (r + 1) * LANES)
        logw.append(
            prior_t[:, r : r + 1] - 0.5 * jnp.sum(acc[part, :], axis=1, keepdims=True)
        )
    top = functools.reduce(jnp.maximum, logw)
    top = jnp.max(top, axis=0, keepdims=True)
    mass = jnp.zeros((LANES, 1), F32)
    mean = jnp.zeros((1, width), F32)
    for r in range(blocks):
        part = slice(r * LANES, (r + 1) * LANES)
        expw = jnp.exp(logw[r] - top)
        mass = mass + expw
        mean = mean + jnp.sum(expw * state[part, :], axis=0, keepdims=True)
    mass = jnp.sum(mass, axis=0, keepdims=True)
    cells = [mean[:, q : q + LANES] for q in range(0, width, LANES)]
    cells.append(jnp.broadcast_to(top, (1, LANES)))
    cells += [jnp.broadcast_to(mass, (1, LANES))] * 3
    stats[me] = jnp.concatenate(cells, axis=0)

    def tell(k, carry):
        other = lax.rem(me + k, n)
        pltpu.make_async_remote_copy(
            src_ref=stats.at[me],
            dst_ref=stats.at[me],
            send_sem=stat_send,
            recv_sem=stat_recv,
            device_id=(other // npair, lax.rem(other, npair)),
            device_id_type=MESH,
        ).start()
        return carry

    lax.fori_loop(1, n, tell, 0)

    source_t = source.T
    wide_in = lax.broadcasted_iota(jnp.int32, (1, n_pad), 1).astype(F32) + float(rows)
    for r in range(blocks):
        part = slice(r * LANES, (r + 1) * LANES)
        col = source_t[:, r : r + 1]
        pick[part, :] = jnp.where(col == wide, 1.0, 0.0).astype(BF16)
        pick_in[part, :] = jnp.where(col == wide_in, 1.0, 0.0).astype(BF16)
    for c in range(rows // CHUNK):
        part = slice(c * CHUNK, (c + 1) * CHUNK)
        out_ref[part, :] = jnp.dot(
            pick[part, :], hi[...], preferred_element_type=F32
        ) + jnp.dot(pick[part, :], lo[...], preferred_element_type=F32)

    if n_pad > n_in:
        rhi[n_in:, :] = jnp.zeros((n_pad - n_in, width), BF16)
        rlo[n_in:, :] = jnp.zeros((n_pad - n_in, width), BF16)
    for group in ((0,), (2, 1)):
        parts = []
        for q in group:
            moves[q].wait()
            parts.append(slice(spans[q][0], spans[q][0] + spans[q][1]))
        for part in parts:
            rhi[part, :] = rin[part, :].astype(BF16)
        for t in range(steps):
            for part in parts:
                advance(t, rin, rhi, rlo, part)
    for c in range(rows // CHUNK):
        part = slice(c * CHUNK, (c + 1) * CHUNK)
        out_ref[part, :] += jnp.dot(
            pick_in[part, :], rhi[...], preferred_element_type=F32
        ) + jnp.dot(pick_in[part, :], rlo[...], preferred_element_type=F32)

    others = stats.at[pl.ds(0, n - 1)]
    pltpu.make_async_copy(others, others, stat_send).wait()
    pltpu.make_async_copy(others, others, stat_recv).wait()
    lines = width // LANES
    shares = stats[...]
    tops = shares[:, lines : lines + 1, :]
    peak = jnp.max(tops, axis=0, keepdims=True)
    scaled = jnp.exp(tops - peak) * shares
    summed = jnp.sum(scaled, axis=0)
    total = summed[lines + 1 : lines + 2, :]
    mean_ref[...] = summed[:lines, :] / total

    def group_weight(device):
        share = stats[device]
        part_sum = share[lines + 1 : lines + 2, :] * jnp.exp(
            share[lines : lines + 1, :] - peak[0]
        )
        return jnp.log(jnp.maximum(float(n) * part_sum / total, 0.1))

    own = group_weight(me)
    cyc_w = group_weight(lax.rem(b + nb - 1, nb) * npair + p)
    pair_w = group_weight(b * npair + lax.rem(p + npair - npair // 2, npair))
    glw_ref[...] = jnp.where(
        source < float(rows),
        own,
        jnp.where(source < float(rows + n_cyc), cyc_w, pair_w),
    )


def per_device(nb, npair, *arrays):
    (particles, prior, trans, drive, current, decay, obsm, weight, observed, anc, cyc, pair) = arrays
    rows, width = particles.shape
    n = nb * npair
    n_in = cyc.shape[0] + pair.shape[0]
    n_pad = -(-n_in // LANES) * LANES
    vmem = pl.BlockSpec(memory_space=pltpu.VMEM)
    smem = pl.BlockSpec(memory_space=pltpu.SMEM)
    hbm = pl.BlockSpec(memory_space=pl.ANY)
    migrated, glw, mean = pl.pallas_call(
        functools.partial(kernel, nb, npair),
        out_shape=(
            jax.ShapeDtypeStruct((rows, width), F32),
            jax.ShapeDtypeStruct((rows // LANES, LANES), F32),
            jax.ShapeDtypeStruct((width // LANES, LANES), F32),
        ),
        in_specs=[hbm, vmem, hbm, vmem, smem, vmem, hbm, vmem, vmem, vmem, vmem, vmem],
        out_specs=(vmem, vmem, vmem),
        scratch_shapes=[
            pltpu.VMEM((rows, width), F32),
            pltpu.VMEM((rows, width), BF16),
            pltpu.VMEM((rows, width), BF16),
            pltpu.VMEM(trans.shape, BF16),
            pltpu.VMEM(obsm.shape, BF16),
            pltpu.VMEM((rows, obsm.shape[1]), F32),
            pltpu.VMEM((rows, rows), BF16),
            pltpu.VMEM((rows, n_pad), BF16),
            pltpu.VMEM((n_in, width), F32),
            pltpu.VMEM((n_pad, width), F32),
            pltpu.VMEM((n_pad, width), BF16),
            pltpu.VMEM((n_pad, width), BF16),
            pltpu.VMEM((n, 8, LANES), F32),
            pltpu.SemaphoreType.DMA((rows // CHUNK + 2,)),
            pltpu.SemaphoreType.DMA((3,)),
            pltpu.SemaphoreType.DMA((3,)),
            pltpu.SemaphoreType.DMA,
            pltpu.SemaphoreType.DMA,
        ],
        compiler_params=pltpu.CompilerParams(
            collective_id=0, has_side_effects=True, vmem_limit_bytes=48 * 2**20
        ),
    )(
        particles,
        prior.reshape(rows // LANES, LANES),
        trans,
        drive.reshape(1, width),
        current,
        decay.reshape(1, width),
        obsm,
        weight.reshape(1, -1),
        observed,
        anc.reshape(rows // LANES, LANES),
        cyc.reshape(-1, LANES),
        pair.reshape(1, -1),
    )
    return migrated, glw.reshape(rows), mean.reshape(width)


def solution(mesh):
    shard, rep = P(("blk", "pair")), P()
    rows = P(("blk", "pair"), None)
    return jax.shard_map(
        functools.partial(per_device, mesh.shape["blk"], mesh.shape["pair"]),
        mesh=mesh,
        in_specs=(rows, shard, rep, rep, rep, rep, rep, rep, rep, shard, shard, shard),
        out_specs=(rows, shard, rep),
        check_vma=False,
    )
```

time: 133 us -> 33 us (0.25)
  blocking collectives: 82.7 us -> 0 us
  Pallas kernels: 0 us -> 19.8 us
  local copies, waits for them, and re-layouts: 23.7 us -> 12.1 us
  matrix products: 8.26 us -> 0 us
  starting transfers between devices: 6.8 us -> 0 us
  other arithmetic: 6.42 us -> 0 us
  waiting for transfers between devices: 2.34 us -> 0 us
  between operations: 2.23 us -> 0.66 us
    pmax x1 -> x0, blocking collectives: 42.1 us -> none  [per_device(): peak = lax.pmax(jnp.max(logw), ('blk', 'pair'))]
    psum x1 -> x0, blocking collectives: 40.6 us -> none  [per_device(): total, summed = lax.psum((local_sum, weighted), ('blk', 'pair'))]
    pallas_call x0 -> x1, Pallas kernels: none -> 19.8 us  [per_device(): pl.pallas_call(functools.partial(kernel, nb, npair), out_shape=(jax.Shape...]
    unnamed x18 -> x27, local copies, waits for them, and re-layouts: 0.34 us -> 12.1 us
    scatter x4 -> x0, local copies, waits for them, and re-layouts: 9.93 us -> none  [the longest x2 7.84 us: per_device(): migrated = resampled.at[cycle_pick].set(cycle_in).at[pair_pick].set(pair_in)]
    gather x3 -> x0, local copies, waits for them, and re-layouts: 9.91 us -> none  [the longest x1 4.87 us: per_device(): resampled = state[ancestors]]
    dot_general x9 -> x0, matrix products: 8.26 us -> none  [the longest x4 5.18 us: per_device(): jnp.dot(rounded, transition, preferred_element_type=jnp.float32)]
    ppermute x4 -> x0, starting transfers between devices: 6.8 us -> none  [shifted(): return lax.ppermute(block, axis, route)]
  transfers between devices with their start and end apart: 4 -> 0, of which waited for: 1 -> 0; matrix products, arithmetic and copies ran while one was open for 14% -> 0% of each run, Pallas kernels for 0% -> 0%
where the time goes in v1:
time: 33 us; the launch traced here: 32.6 us
  Pallas kernels  19.8 us (60%)
  local copies, waits for them, and re-layouts  12.1 us (37%)
  between operations  0.66 us (2%)
    pallas_call x1, Pallas kernels, per_device(): pl.pallas_call(functools.partial(kernel, nb, npair), out_shape=(jax.Shape...  19.8 us
    unnamed x27, local copies, waits for them, and re-layouts  12.1 us

profile of v1, /device:TPU:0, one launch (start us, length us, event | category | flops | bytes accessed | tf_op | source)
XLA Modules:
  0.0 32.6 jit_solution(2162541113695353353)
XLA Ops:
  0.6 0.0 copy-start
  0.6 1.6 %copy-done = f32[1024,512]{1,0:T(8,128)S(1)} copy-done((f32[1024,512]{1,0:T(8,128)S(1)}, f32[1024,512]{1,0:T(8,128)}, u32[]{:S(2)}) %copy-start) | copy-done | bytes 2097176
  2.2 0.0 copy-start.1
  2.2 1.0 %copy-done.1 = bf16[512,512]{1,0:T(8,128)(2,1)S(1)} copy-done((bf16[512,512]{1,0:T(8,128)(2,1)S(1)}, bf16[512,512]{1,0:T(8,128)(2,1)}, u32[]{:S(2)}) %copy-start.1) | copy-done | bytes 524312
  3.3 0.0 copy-start.2
  3.3 0.9 %copy-done.2 = bf16[512,128]{1,0:T(8,128)(2,1)S(1)} copy-done((bf16[512,128]{1,0:T(8,128)(2,1)S(1)}, bf16[512,128]{1,0:T(8,128)(2,1)}, u32[]{:S(2)}) %copy-start.2) | copy-done | bytes 131096
  4.2 0.0 copy-start.3
  4.2 0.7 %copy-done.3 = f32[1024]{0:T(1024)S(1)} copy-done((f32[1024]{0:T(1024)S(1)}, f32[1024]{0:T(1024)}, u32[]{:S(2)}) %copy-start.3) | copy-done | bytes 4120
  4.9 0.0 copy-start.4
  4.9 0.7 %copy-done.4 = s32[1024]{0:T(1024)S(1)} copy-done((s32[1024]{0:T(1024)S(1)}, s32[1024]{0:T(1024)}, u32[]{:S(2)}) %copy-start.4) | copy-done | bytes 4120
  5.5 0.0 copy-start.5
  5.6 0.7 %copy-done.5 = f32[512]{0:T(512)S(1)} copy-done((f32[512]{0:T(512)S(1)}, f32[512]{0:T(512)}, u32[]{:S(2)}) %copy-start.5) | copy-done | bytes 2072
  6.2 0.0 copy-start.6
  6.2 0.7 %copy-done.6 = f32[512]{0:T(512)S(1)} copy-done((f32[512]{0:T(512)S(1)}, f32[512]{0:T(512)}, u32[]{:S(2)}) %copy-start.6) | copy-done | bytes 2072
  6.9 0.0 copy-start.7
  6.9 0.7 %copy-done.7 = f32[4,128]{1,0:T(4,128)S(1)} copy-done((f32[4,128]{1,0:T(4,128)S(1)}, f32[4,128]{1,0:T(4,128)}, u32[]{:S(2)}) %copy-start.7) | copy-done | bytes 2072
  7.6 0.7 %copy-done.8 = s32[256]{0:T(256)S(1)} copy-done((s32[256]{0:T(256)S(1)}, s32[256]{0:T(256)}, u32[]{:S(2)}) %copy-start.8) | copy-done | bytes 1048
  8.3 0.7 %copy-done.9 = f32[4]{0:T(128)S(1)} copy-done((f32[4]{0:T(128)S(1)}, f32[4]{0:T(128)}, u32[]{:S(2)}) %copy-start.9) | copy-done | bytes 40
  8.9 0.7 %copy-done.10 = f32[128]{0:T(128)S(1)} copy-done((f32[128]{0:T(128)S(1)}, f32[128]{0:T(128)}, u32[]{:S(2)}) %copy-start.10) | copy-done | bytes 536
  9.6 0.7 %copy-done.11 = s32[32]{0:T(128)S(1)} copy-done((s32[32]{0:T(128)S(1)}, s32[32]{0:T(128)}, u32[]{:S(2)}) %copy-start.11) | copy-done | bytes 152
  10.2 19.8 %shard_map.139 = (f32[1024,512]{1,0:T(8,128)S(1)}, f32[8,128]{1,0:T(8,128)S(1)}, f32[4,128]{1,0:T(4,128)S(1)}) custom-call(f32[1024,512]{1,0:T(8,128)S(1)} %copy-done, f32[8,128]{1,0:T(8,128)S(1)} %bitcast.9, bf16[512,512]{1,0:T(8,128)(2,1)S(1)} %copy-done.1, f32[1,512]{1,0:T(1,128)S(1)} %bitcast.12, f32[4]{0:T(128)S(1)} %copy-done.9, ...), custom_call_target="tpu_custom_call" | custom-call | tf_op jit(solution)/shard_map/pallas_call | solution.py:275
  30.1 1.3 %copy.18 = f32[1024,512]{1,0:T(8,128)} copy(f32[1024,512]{1,0:T(8,128)S(1)} %get-tuple-element.12) | data formatting | bytes 4194304
  31.4 0.6 %copy.19 = f32[1024]{0:T(1024)} copy(f32[1024]{0:T(1024)S(1)} %bitcast.11) | data formatting | bytes 8192
  32.0 0.6 %copy.20 = f32[512]{0:T(512)} copy(f32[512]{0:T(512)S(1)} %bitcast.14) | data formatting | bytes 4096
  (4 shorter events, 0.0 us)
Async XLA Ops:
  0.6 1.6 %copy-start = (f32[1024,512]{1,0:T(8,128)S(1)}, f32[1024,512]{1,0:T(8,128)}, u32[]{:S(2)}) copy-start(f32[1024,512]{1,0:T(8,128)} %part_hbm.1) | copy-start | bytes 6291460
  2.2 1.0 %copy-start.1 = (bf16[512,512]{1,0:T(8,128)(2,1)S(1)}, bf16[512,512]{1,0:T(8,128)(2,1)}, u32[]{:S(2)}) copy-start(bf16[512,512]{1,0:T(8,128)(2,1)} %trans_hbm.1) | copy-start | bytes 1572868
  3.3 0.9 %copy-start.2 = (bf16[512,128]{1,0:T(8,128)(2,1)S(1)}, bf16[512,128]{1,0:T(8,128)(2,1)}, u32[]{:S(2)}) copy-start(bf16[512,128]{1,0:T(8,128)(2,1)} %obsm_hbm.1) | copy-start | bytes 393220
  4.2 0.7 %copy-start.3 = (f32[1024]{0:T(1024)S(1)}, f32[1024]{0:T(1024)}, u32[]{:S(2)}) copy-start(f32[1024]{0:T(1024)} %param.13) | copy-start | bytes 12292
  4.9 0.7 %copy-start.4 = (s32[1024]{0:T(1024)S(1)}, s32[1024]{0:T(1024)}, u32[]{:S(2)}) copy-start(s32[1024]{0:T(1024)} %param.21) | copy-start | bytes 12292
  5.5 0.7 %copy-start.5 = (f32[512]{0:T(512)S(1)}, f32[512]{0:T(512)}, u32[]{:S(2)}) copy-start(f32[512]{0:T(512)} %param.15) | copy-start | bytes 6148
  6.2 0.7 %copy-start.6 = (f32[512]{0:T(512)S(1)}, f32[512]{0:T(512)}, u32[]{:S(2)}) copy-start(f32[512]{0:T(512)} %param.17) | copy-start | bytes 6148
  6.9 0.7 %copy-start.7 = (f32[4,128]{1,0:T(4,128)S(1)}, f32[4,128]{1,0:T(4,128)}, u32[]{:S(2)}) copy-start(f32[4,128]{1,0:T(4,128)} %obs_ref.1) | copy-start | bytes 6148
  7.6 0.7 %copy-start.8 = (s32[256]{0:T(256)S(1)}, s32[256]{0:T(256)}, u32[]{:S(2)}) copy-start(s32[256]{0:T(256)} %param.22) | copy-start | bytes 3076
  8.3 0.7 %copy-start.9 = (f32[4]{0:T(128)S(1)}, f32[4]{0:T(128)}, u32[]{:S(2)}) copy-start(f32[4]{0:T(128)} %cur_ref.1) | copy-start | bytes 52
  8.9 0.7 %copy-start.10 = (f32[128]{0:T(128)S(1)}, f32[128]{0:T(128)}, u32[]{:S(2)}) copy-start(f32[128]{0:T(128)} %param.19) | copy-start | bytes 1540
  9.6 0.7 %copy-start.11 = (s32[32]{0:T(128)S(1)}, s32[32]{0:T(128)}, u32[]{:S(2)}) copy-start(s32[32]{0:T(128)} %param.23) | copy-start | bytes 388

commit v2 on v1

--- a/solution.py
+++ b/solution.py
@@ -12,6 +12,8 @@
 BF16 = jnp.bfloat16
 LANES = 128
 CHUNK = 256
+STEP_CHUNK = 1024
+PICK_CHUNK = 512
 
 
 def column(row_block):
@@ -23,23 +25,22 @@
     nb,
     npair,
     part_hbm,
-    prior_ref,
     trans_hbm,
-    drive_ref,
-    cur_ref,
-    decay_ref,
     obsm_hbm,
-    weight_ref,
-    obs_ref,
-    anc_ref,
-    cyc_ref,
-    pair_ref,
+    anc_hbm,
+    cyc_hbm,
+    pair_hbm,
+    prior_hbm,
+    drive_hbm,
+    cur_hbm,
+    decay_hbm,
+    weight_hbm,
+    obs_hbm,
     out_ref,
     glw_ref,
     mean_ref,
     state,
     hi,
-    lo,
     trans,
     obsm,
     acc,
@@ -48,9 +49,18 @@
     rout,
     rin,
     rhi,
-    rlo,
     stats,
+    anc_ref,
+    cyc_ref,
+    pair_ref,
+    prior_ref,
+    drive_ref,
+    cur_ref,
+    decay_ref,
+    weight_ref,
+    obs_ref,
     load_sem,
+    small_sem,
     send_sem,
     recv_sem,
     stat_send,
@@ -68,6 +78,22 @@
     n_in = n_cyc + n_pair
     n_pad = rin.shape[0]
 
+    small = []
+    for q, (src, dst) in enumerate(
+        (
+            (anc_hbm, anc_ref),
+            (cyc_hbm, cyc_ref),
+            (pair_hbm, pair_ref),
+            (prior_hbm, prior_ref),
+            (drive_hbm, drive_ref),
+            (cur_hbm, cur_ref),
+            (decay_hbm, decay_ref),
+            (weight_hbm, weight_ref),
+            (obs_hbm, obs_ref),
+        )
+    ):
+        small.append(pltpu.make_async_copy(src, dst, small_sem.at[q]))
+        small[-1].start()
     loads = []
     for c in range(rows // CHUNK):
         part = pl.ds(c * CHUNK, CHUNK)
@@ -94,6 +120,9 @@
         return carry
 
     lax.fori_loop(1, n, greet, 0)
+
+    for copy in small:
+        copy.wait()
 
     anc = anc_ref[...].astype(F32)
     picks = [column(cyc_ref[q : q + 1, :].astype(F32)) for q in range(n_cyc // LANES)]
@@ -124,8 +153,7 @@
     pl.semaphore_wait(barrier, n - 1)
     right = lax.rem(b + 1, nb)
     across = lax.rem(p + npair // 2, npair)
-    half = n_cyc // 2
-    spans = [(0, half, (right, p)), (half, half, (right, p)), (n_cyc, n_pair, (b, across))]
+    spans = [(0, n_cyc, (right, p)), (n_cyc, n_pair, (b, across))]
     moves = []
     for q, (start, size, target) in enumerate(spans):
         part = pl.ds(start, size)
@@ -144,21 +172,19 @@
     load_o.wait()
     decay = decay_ref[...]
 
-    def advance(t, st, h, l, part):
+    def advance(t, st, h, part):
         drift = jnp.dot(h[part, :], trans[...], preferred_element_type=F32)
-        drift = drift + cur_ref[t] * drive_ref[...]
+        drift = drift + cur_ref[0:1, t : t + 1] * drive_ref[...]
         new = decay * st[part, :] + jnp.tanh(drift)
         rounded = new.astype(BF16)
         st[part, :] = new
         h[part, :] = rounded
-        if t == steps - 1:
-            l[part, :] = (new - rounded.astype(F32)).astype(BF16)
         return rounded
 
     for t in range(steps):
-        for c in range(rows // CHUNK):
-            part = slice(c * CHUNK, (c + 1) * CHUNK)
-            rounded = advance(t, state, hi, lo, part)
+        for c in range(rows // STEP_CHUNK):
+            part = slice(c * STEP_CHUNK, (c + 1) * STEP_CHUNK)
+            rounded = advance(t, state, hi, part)
             predicted = jnp.dot(rounded, obsm[...], preferred_element_type=F32)
             misfit = predicted - obs_ref[t : t + 1, :]
             cost = weight_ref[...] * misfit * misfit
@@ -209,30 +235,20 @@
         col = source_t[:, r : r + 1]
         pick[part, :] = jnp.where(col == wide, 1.0, 0.0).astype(BF16)
         pick_in[part, :] = jnp.where(col == wide_in, 1.0, 0.0).astype(BF16)
-    for c in range(rows // CHUNK):
-        part = slice(c * CHUNK, (c + 1) * CHUNK)
-        out_ref[part, :] = jnp.dot(
-            pick[part, :], hi[...], preferred_element_type=F32
-        ) + jnp.dot(pick[part, :], lo[...], preferred_element_type=F32)
-
     if n_pad > n_in:
         rhi[n_in:, :] = jnp.zeros((n_pad - n_in, width), BF16)
-        rlo[n_in:, :] = jnp.zeros((n_pad - n_in, width), BF16)
-    for group in ((0,), (2, 1)):
-        parts = []
-        for q in group:
-            moves[q].wait()
-            parts.append(slice(spans[q][0], spans[q][0] + spans[q][1]))
-        for part in parts:
-            rhi[part, :] = rin[part, :].astype(BF16)
-        for t in range(steps):
-            for part in parts:
-                advance(t, rin, rhi, rlo, part)
-    for c in range(rows // CHUNK):
-        part = slice(c * CHUNK, (c + 1) * CHUNK)
+    for move in moves:
+        move.wait()
+    part_in = slice(0, n_in)
+    rhi[part_in, :] = rin[part_in, :].astype(BF16)
+    for t in range(steps):
+        advance(t, rin, rhi, part_in)
+    for c in range(rows // PICK_CHUNK):
+        part = slice(c * PICK_CHUNK, (c + 1) * PICK_CHUNK)
+        out_ref[part, :] = jnp.dot(pick[part, :], hi[...], preferred_element_type=F32)
         out_ref[part, :] += jnp.dot(
             pick_in[part, :], rhi[...], preferred_element_type=F32
-        ) + jnp.dot(pick_in[part, :], rlo[...], preferred_element_type=F32)
+        )
 
     others = stats.at[pl.ds(0, n - 1)]
     pltpu.make_async_copy(others, others, stat_send).wait()
@@ -270,8 +286,18 @@
     n_in = cyc.shape[0] + pair.shape[0]
     n_pad = -(-n_in // LANES) * LANES
     vmem = pl.BlockSpec(memory_space=pltpu.VMEM)
-    smem = pl.BlockSpec(memory_space=pltpu.SMEM)
     hbm = pl.BlockSpec(memory_space=pl.ANY)
+    small = (
+        anc.reshape(rows // LANES, LANES),
+        cyc.reshape(-1, LANES),
+        pair.reshape(1, -1),
+        prior.reshape(rows // LANES, LANES),
+        drive.reshape(1, width),
+        current.reshape(1, -1),
+        decay.reshape(1, width),
+        weight.reshape(1, -1),
+        observed,
+    )
     migrated, glw, mean = pl.pallas_call(
         functools.partial(kernel, nb, npair),
         out_shape=(
@@ -279,11 +305,10 @@
             jax.ShapeDtypeStruct((rows // LANES, LANES), F32),
             jax.ShapeDtypeStruct((width // LANES, LANES), F32),
         ),
-        in_specs=[hbm, vmem, hbm, vmem, smem, vmem, hbm, vmem, vmem, vmem, vmem, vmem],
+        in_specs=[hbm] * 12,
         out_specs=(vmem, vmem, vmem),
         scratch_shapes=[
             pltpu.VMEM((rows, width), F32),
-            pltpu.VMEM((rows, width), BF16),
             pltpu.VMEM((rows, width), BF16),
             pltpu.VMEM(trans.shape, BF16),
             pltpu.VMEM(obsm.shape, BF16),
@@ -293,32 +318,46 @@
             pltpu.VMEM((n_in, width), F32),
             pltpu.VMEM((n_pad, width), F32),
             pltpu.VMEM((n_pad, width), BF16),
-            pltpu.VMEM((n_pad, width), BF16),
             pltpu.VMEM((n, 8, LANES), F32),
+            *[pltpu.VMEM(x.shape, x.dtype) for x in small],
             pltpu.SemaphoreType.DMA((rows // CHUNK + 2,)),
-            pltpu.SemaphoreType.DMA((3,)),
-            pltpu.SemaphoreType.DMA((3,)),
+            pltpu.SemaphoreType.DMA((len(small),)),
+            pltpu.SemaphoreType.DMA((2,)),
+            pltpu.SemaphoreType.DMA((2,)),
             pltpu.SemaphoreType.DMA,
             pltpu.SemaphoreType.DMA,
         ],
         compiler_params=pltpu.CompilerParams(
-            collective_id=0, has_side_effects=True, vmem_limit_bytes=48 * 2**20
+            collective_id=0, has_side_effects=True, vmem_limit_bytes=64 * 2**20
         ),
-    )(
-        particles,
-        prior.reshape(rows // LANES, LANES),
-        trans,
-        drive.reshape(1, width),
-        current,
-        decay.reshape(1, width),
-        obsm,
-        weight.reshape(1, -1),
-        observed,
-        anc.reshape(rows // LANES, LANES),
-        cyc.reshape(-1, LANES),
-        pair.reshape(1, -1),
-    )
+    )(particles, trans, obsm, *small)
+    migrated, glw, mean = write_out(migrated, glw, mean)
     return migrated, glw.reshape(rows), mean.reshape(width)
+
+
+def write_kernel(a, b, c, a_out, b_out, c_out):
+    a_out[...] = a[...]
+    b_out[...] = b[...]
+    c_out[...] = c[...]
+
+
+def write_out(migrated, glw, mean):
+    rows, width = migrated.shape
+    specs = [
+        pl.BlockSpec((CHUNK, width), lambda i: (i, 0)),
+        pl.BlockSpec(glw.shape, lambda i: (0, 0)),
+        pl.BlockSpec(mean.shape, lambda i: (0, 0)),
+    ]
+    return pl.pallas_call(
+        write_kernel,
+        grid=(rows // CHUNK,),
+        out_shape=tuple(
+            jax.ShapeDtypeStruct(x.shape, x.dtype) for x in (migrated, glw, mean)
+        ),
+        in_specs=specs,
+        out_specs=tuple(specs),
+        compiler_params=pltpu.CompilerParams(vmem_limit_bytes=64 * 2**20),
+    )(migrated, glw, mean)
 
 
 def solution(mesh):

time: 33 us -> 24.4 us (0.74)
  local copies, waits for them, and re-layouts: 12.1 us -> 0 us
  Pallas kernels: 19.8 us -> 23.5 us
    unnamed x27 -> x0, local copies, waits for them, and re-layouts: 12.1 us -> none
    pallas_call x0 -> x1, Pallas kernels: none -> 3.8 us  [write_out(): pl.pallas_call(write_kernel, grid=(rows // CHUNK,), out_shape=tuple((jax....]
where the time goes in v2:
time: 24.4 us; the launch traced here: 24.2 us
  Pallas kernels  23.5 us (96%)
  between operations  0.64 us (3%)
    pallas_call x1, Pallas kernels, per_device(): pl.pallas_call(functools.partial(kernel, nb, npair), out_shape=(jax.Shape...  19.7 us
    pallas_call x1, Pallas kernels, write_out(): pl.pallas_call(write_kernel, grid=(rows // CHUNK,), out_shape=tuple((jax....  3.8 us

profile of v2, /device:TPU:0, one launch (start us, length us, event | category | flops | bytes accessed | tf_op | source)
XLA Modules:
  0.0 24.2 jit_solution(15066644737846844707)
XLA Ops:
  0.6 19.7 %shard_map.139 = (f32[1024,512]{1,0:T(8,128)}, f32[8,128]{1,0:T(8,128)}, f32[4,128]{1,0:T(4,128)}) custom-call(f32[1024,512]{1,0:T(8,128)} %part_hbm.1, bf16[512,512]{1,0:T(8,128)(2,1)} %trans_hbm.1, bf16[512,128]{1,0:T(8,128)(2,1)} %obsm_hbm.1, s32[8,128]{1,0:T(8,128)} %bitcast.10, s32[2,128]{1,0:T(2,128)} %bitcast.14, s32[1,32]{1,0:T(1,128)} %bitcast.15, ...), custom_call_target="tpu_custom_call" | custom-call | tf_op jit(solution)/shard_map/pallas_call | solution.py:301
  20.4 3.8 %shard_map.140 = (f32[1024,512]{1,0:T(8,128)}, f32[8,128]{1,0:T(8,128)}, f32[4,128]{1,0:T(4,128)}) custom-call(f32[1024,512]{1,0:T(8,128)} %get-tuple-element.9.a, f32[8,128]{1,0:T(8,128)} %get-tuple-element.10.b, f32[4,128]{1,0:T(4,128)} %get-tuple-element.11.c), custom_call_target="tpu_custom_call" | custom-call | tf_op jit(solution)/shard_map/pallas_call | solution.py:351
